TPU v7x, 512 devices: a whole 4x4x16 slice. The times are simulated.
512 devices in a mesh: row: 32 (over x, y, core), col: 16 (over z).
Axes of the slice: x: 4, y: 4, z: 16, core: 2. Of those that a mesh axis runs over, the one named last changes fastest.
Arguments:
- hessian: float32 [2, 8192, 4, 4096], P(None, 'row', None, 'col'), as said below
- masses: float32 [16384], replicated, may hold values from 1 to 32
- shift: float32 [1], replicated, may hold values from 1 to 4
Outputs:
- factored: float32 [2, 8192, 4, 4096], P(None, 'row', None, 'col')
Inputs may be any that keep to these rules, and one draw needn't show every extreme that they name: `hessian`: symmetric and positive definite.
All inputs are finite; a program needn't handle non-finite values.
Results may differ from a plain program's by a relative error of at most 0.0001.
Values sent between devices are 32-bit elements; how exact they have to be, the bound alone decides.
A program may use at most 64 MiB of HBM per device.

v0:
```python
import jax
import jax.numpy as jnp
from jax import lax
from jax.sharding import PartitionSpec as P

PANELS = 2


def from_root(block, axis, holder):
    block = jnp.where(lax.axis_index(axis) == holder, block, jnp.zeros_like(block))
    return lax.psum(block, axis)


def shards(hessian, masses, shift):
    row_count = lax.axis_size("row")
    col_count = lax.axis_size("col")
    row_index = lax.axis_index("row")
    col_index = lax.axis_index("col")
    row_blocks, block_size, col_blocks, _ = hessian.shape
    row_mass = lax.dynamic_index_in_dim(
        masses.reshape(row_blocks, row_count, block_size), row_index, 1, keepdims=False
    )
    col_mass = lax.dynamic_index_in_dim(
        masses.reshape(col_blocks, col_count, block_size), col_index, 1, keepdims=False
    )
    row_weight = 1.0 / jnp.sqrt(row_mass)
    col_weight = 1.0 / jnp.sqrt(col_mass)
    row_global = jnp.arange(row_blocks) * row_count + row_index
    col_global = jnp.arange(col_blocks) * col_count + col_index
    offsets = jnp.arange(block_size)
    row_cells = row_global[:, None] * block_size + offsets[None, :]
    col_cells = col_global[:, None] * block_size + offsets[None, :]
    on_diagonal = row_cells[:, :, None, None] == col_cells[None, None, :, :]
    matrix = hessian * row_weight[:, :, None, None] * col_weight[None, None, :, :]
    matrix = matrix + jnp.where(on_diagonal, shift[0], 0.0)
    pending = None
    for panel in range(PANELS):
        row_slot = panel // row_count
        row_owner = panel % row_count
        col_slot = panel // col_count
        col_owner = panel % col_count
        column_source = matrix[:, :, col_slot, :]
        row_source = matrix[row_slot]
        pending = None
        column = from_root(column_source, "col", col_owner)
        across_rows = from_root(row_source, "row", row_owner)
        pivot = from_root(
            row_source[:, col_slot, :], ("row", "col"), row_owner * col_count + col_owner
        )
        factor = jnp.linalg.cholesky(pivot)
        below = lax.linalg.triangular_solve(
            factor,
            column.reshape(row_blocks * block_size, block_size),
            left_side=False,
            lower=True,
            transpose_a=True,
        )
        across = lax.linalg.triangular_solve(
            factor,
            across_rows.reshape(block_size, col_blocks * block_size),
            left_side=True,
            lower=True,
        )
        row_later = jnp.repeat(row_global > panel, block_size)
        col_later = jnp.repeat(col_global > panel, block_size)
        below_used = jnp.where(row_later[:, None], below, 0.0)
        across_used = jnp.where(col_later[None, :], across, 0.0)
        product = jnp.dot(below_used, across_used, precision=lax.Precision.HIGHEST)
        matrix = matrix - product.reshape(row_blocks, block_size, col_blocks, block_size)
        block_rows = row_global[:, None, None]
        placed = jnp.where(
            block_rows > panel,
            below.reshape(row_blocks, block_size, block_size),
            jnp.where(block_rows == panel, factor[None, :, :], 0.0),
        )
        matrix = matrix.at[:, :, col_slot, :].set(
            jnp.where(col_index == col_owner, placed, matrix[:, :, col_slot, :])
        )
        cleared = jnp.where(
            (row_index == row_owner) & (col_global > panel)[None, :, None], 0.0, matrix[row_slot]
        )
        matrix = matrix.at[row_slot].set(cleared)
    return matrix


def solution(mesh):
    placed = (P(None, "row", None, "col"), P(), P())
    return jax.shard_map(
        shards, mesh=mesh, in_specs=placed, out_specs=P(None, "row", None, "col"), check_vma=False
    )
```

profile of v0, /device:TPU:1, one launch (start us, length us, event | category | flops | bytes accessed | tf_op | source)
XLA Modules:
  0.0 1523.1 jit_solution(5979681432682516066)
XLA Ops:
  8.5 1.9 copy.10
  17.6 457.8 %all-reduce.8.cloned.1.call-done = f32[256,256]{0,1:T(8,128)} async-done(((f32[256,256]{0,1:T(8,128)}), f32[256,256]{0,1:T(8,128)}) %all-reduce.8.cloned.1.call-update) | async-done | bytes 262160 | tf_op jit(solution)/shard_map/psum | solution.py:11
  477.4 11.7 cholesky.130
  489.2 9.8 custom-call.17
  499.5 11.7 cholesky.147
  513.4 4.6 while.12
  517.9 19.7 %custom-call.18 = f32[2,128,128]{1,2,0:T(8,128)S(1)} custom-call(f32[2,128,128]{2,1,0:T(8,128)S(1)} %get-tuple-element.84), custom_call_target="InvertDiagBlocksLowerTriangular" | custom-call | tf_op jit(solution)/shard_map/triangular_solve/custom-call.0 | solution.py:51
  537.7 64.8 %all-reduce.10.cloned.1.call-done = f32[512,256]{1,0:T(8,128)} async-done(((f32[512,256]{1,0:T(8,128)}), f32[512,256]{1,0:T(8,128)}) %all-reduce.10.cloned.1.call-update) | async-done | bytes 524304 | tf_op jit(solution)/shard_map/psum | solution.py:11
  606.3 141.2 %all-reduce.12.cloned.1.call-done = f32[256,1024]{0,1:T(8,128)} async-done(((f32[256,1024]{0,1:T(8,128)}), f32[256,1024]{0,1:T(8,128)}) %all-reduce.12.cloned.1.call-update) | async-done | bytes 1048592 | tf_op jit(solution)/shard_map/psum | solution.py:11
  747.5 1.7 fusion.11
  749.2 2.0 convolution_subtract_fusion.1
  751.9 1.9 fusion.1
  753.8 2.0 reshape.324
  755.8 2.9 copy.13
  758.7 2.7 fusion.67
  765.9 453.7 %all-reduce.14.cloned.1.call-done = f32[256,256]{0,1:T(8,128)} async-done(((f32[256,256]{0,1:T(8,128)}), f32[256,256]{0,1:T(8,128)}) %all-reduce.14.cloned.1.call-update) | async-done | bytes 262160 | tf_op jit(solution)/shard_map/psum | solution.py:11
  1221.6 11.7 cholesky.164
  1233.4 9.8 custom-call.20
  1243.7 11.7 cholesky.181
  1257.9 4.0 while.13
  1261.9 19.7 %custom-call.21 = f32[2,128,128]{1,2,0:T(8,128)S(1)} custom-call(f32[2,128,128]{2,1,0:T(8,128)S(1)} %get-tuple-element.86), custom_call_target="InvertDiagBlocksLowerTriangular" | custom-call | tf_op jit(solution)/shard_map/triangular_solve/custom-call.0 | solution.py:51
  1282.4 64.1 %all-reduce.16.cloned.1.call-done = f32[512,256]{1,0:T(8,128)} async-done(((f32[512,256]{1,0:T(8,128)}), f32[512,256]{1,0:T(8,128)}) %all-reduce.16.cloned.1.call-update) | async-done | bytes 524304 | tf_op jit(solution)/shard_map/psum | solution.py:11
  1353.0 138.7 %all-reduce.18.cloned.1.call-done = f32[256,1024]{0,1:T(8,128)} async-done(((f32[256,1024]{0,1:T(8,128)}), f32[256,1024]{0,1:T(8,128)}) %all-reduce.18.cloned.1.call-update) | async-done | bytes 1048592 | tf_op jit(solution)/shard_map/psum | solution.py:11
  1491.8 1.7 fusion.8
  1493.4 2.0 convolution_subtract_fusion
  1496.1 3.2 fusion.4
  1499.3 3.2 reshape.328
  1502.5 2.9 copy.19
  1505.4 3.3 sub.7
  1508.7 2.0 fusion.7
  1510.7 2.4 fusion
  1513.1 2.9 copy.23
  (113 shorter events, 40.2 us)
Async XLA Ops:
  6.5 468.8 %all-reduce.8.cloned.1.call-start = ((), (), s32[]{:S(2)}) async-start(), calls=%async_computation | async-start | bytes 524288 | tf_op jit(solution)/shard_map/psum | solution.py:11
  10.5 1.3 copy-start
  11.8 1.3 copy-start.1
  13.2 3.0 copy-start.2
  14.0 588.6 %all-reduce.10.cloned.1.call-start = ((), (), s32[]{:S(2)}) async-start(), calls=%async_computation.1 | async-start | bytes 1048576 | tf_op jit(solution)/shard_map/psum | solution.py:11
  16.1 731.4 %all-reduce.12.cloned.1.call-start = ((), (), s32[]{:S(2)}) async-start(), calls=%async_computation.2 | async-start | bytes 2097152 | tf_op jit(solution)/shard_map/psum | solution.py:11
  17.3 1202.3 %all-reduce.14.cloned.1.call-start = ((), (), s32[]{:S(2)}) async-start(), calls=%async_computation.3 | async-start | bytes 524288 | tf_op jit(solution)/shard_map/psum | solution.py:11
  763.7 582.8 %all-reduce.16.cloned.1.call-start = ((), (), s32[]{:S(2)}) async-start(), calls=%async_computation.4 | async-start | bytes 1048576 | tf_op jit(solution)/shard_map/psum | solution.py:11
  764.9 726.9 %all-reduce.18.cloned.1.call-start = ((), (), s32[]{:S(2)}) async-start(), calls=%async_computation.5 | async-start | bytes 2097152 | tf_op jit(solution)/shard_map/psum | solution.py:11
  765.1 0.6 copy-start.5
  1505.4 3.3 copy-start.3
  1505.4 3.3 copy-start.4
  1505.4 3.3 copy-start.6
Sparse Core Ops, SparseCore 0:
  14.1 461.2 all-reduce.7
  477.8 124.7 all-reduce.9
  605.8 141.6 all-reduce.11
  763.9 455.6 all-reduce.13
  1221.7 124.8 all-reduce.15
  1350.0 141.7 all-reduce.17
where the time goes:
time: 1530 us; the launch traced here: 1520 us
  waiting for transfers between devices  1320 us (86%)
  other arithmetic  127 us (8%)
  local copies, waits for them, and re-layouts  35.8 us (2%)
  matrix products  21.3 us (1%)
  between operations  17.3 us (1%)
    psum x6, waiting for transfers between devices, from_root(): return lax.psum(block, axis)  1320 us
    another operation x13, other arithmetic, shards(): factor = jnp.linalg.cholesky(pivot)  68.6 us
    another operation x7, other arithmetic, shards(): lax.linalg.triangular_solve(factor, column.reshape(row_blocks * block_siz...  40.3 us
  transfers between devices with their start and end apart: 6, of which 6 were waited for; matrix products, arithmetic and copies ran while one was open for 9% of the time, Pallas kernels for 0%

commit v1 on v0

v1 whole, which is shorter than its diff:
```python
import functools

import jax
import jax.numpy as jnp
from jax import lax
from jax.experimental import pallas as pl
from jax.experimental.pallas import tpu as pltpu
from jax.sharding import PartitionSpec as P

MESH = pl.DeviceIdType.MESH
HIGHEST = lax.Precision.HIGHEST
Z, R = 16, 32
NB = 256
CHUNKS = 8
ROWS = 512 // CHUNKS
PIVOTS = ((0, 0), (0, 1), (1, 1))


def eight(i):
    return pl.ds(pl.multiple_of(8 * i, 8), 8)


def wait_for(ref, sem):
    pltpu.make_async_copy(ref, ref, sem).wait()


def lane(x, i):
    return jnp.broadcast_to(x[:, i : i + 1], (8, 128))


def sublane(x, i):
    return jnp.broadcast_to(x[i : i + 1, :], (8, x.shape[1]))


def tree_sum(terms):
    while len(terms) > 1:
        terms = [terms[i] + terms[i + 1] for i in range(0, len(terms), 2)]
    return terms[0]


def factor8(tile, off):
    s, low, inv = {}, {}, {}
    for k in range(8):
        column = lane(tile, off + k)
        for i in range(k, 8):
            s[i, k] = sublane(column, i)
    for j in range(8):
        root = lax.rsqrt(s[j, j])
        for i in range(j + 1, 8):
            low[i, j] = s[i, j] * root
        for k in range(j + 1, 8):
            for i in range(k, 8):
                s[i, k] = s[i, k] - low[i, j] * low[k, j]
        inv[j, j] = root
        for c in range(j):
            total = low[j, c] * inv[c, c]
            for k in range(c + 1, j):
                total = total + low[j, k] * inv[k, c]
            inv[j, c] = -(total * root)
    row = lax.broadcasted_iota(jnp.int32, (8, 128), 0)
    columns = []
    for c in range(8):
        x = jnp.zeros((8, 128), jnp.float32)
        for i in range(c, 8):
            x = jnp.where(row == i, inv[i, c], x)
        columns.append(x)
    return columns


def combine(columns, x):
    return tree_sum([columns[j] * sublane(x, j) for j in range(8)])


def factor128(block, upper_ref, inverse_ref, pump):
    rows = lax.broadcasted_iota(jnp.int32, (8, 128), 0)
    lanes = lax.broadcasted_iota(jnp.int32, (8, 128), 1)
    d = [block[8 * t : 8 * t + 8, :] for t in range(16)]
    e = [jnp.where(lanes == rows + 8 * t, 1.0, 0.0) for t in range(16)]
    for t in range(16):
        columns = factor8(d[t], 8 * t)
        u = combine(columns, d[t])
        f = combine(columns, e[t])
        upper_ref[8 * t : 8 * t + 8, :] = jnp.where(lanes >= rows + 8 * t, u, 0.0)
        inverse_ref[8 * t : 8 * t + 8, :] = f
        if t % 4 == 3:
            pump(t // 4)
        if t == 15:
            break
        v = u.T
        ub = [sublane(u, j) for j in range(8)]
        fb = [sublane(f, j) for j in range(8)]
        for q in range(t + 1, 16):
            vq = v[8 * q : 8 * q + 8, :]
            g = [lane(vq, j) for j in range(8)]
            d[q] = d[q] - tree_sum([g[j] * ub[j] for j in range(8)])
            e[q] = e[q] - tree_sum([g[j] * fb[j] for j in range(8)])


def split(x):
    high = x.astype(jnp.bfloat16)
    return high, (x - high.astype(jnp.float32)).astype(jnp.bfloat16)


def dot(a, b):
    return jnp.dot(a, b, preferred_element_type=jnp.float32)


def kernel(x, out, piv, rb, cb, w, ud, md, below, across,
           s_a, r_a, s_b, r_b, s_c, r_c, s_1, r_1, s_2, r_2, s_z, r_z):
    r, z = lax.axis_index("row"), lax.axis_index("col")

    def at_row(i):
        return (lax.rem(r + i, R), z)

    def at_col(i):
        return (r, lax.rem(z + i + Z, Z))

    barrier = pltpu.get_barrier_semaphore()

    def greet_col(i, carry):
        pl.semaphore_signal(barrier, inc=1, device_id=at_col(i), device_id_type=MESH)
        return carry

    def greet_row(i, carry):
        pl.semaphore_signal(barrier, inc=1, device_id=at_row(i), device_id_type=MESH)
        return carry

    lax.fori_loop(1, Z, greet_col, 0)
    lax.fori_loop(1, R, greet_row, 0)
    pl.semaphore_wait(barrier, Z - 1 + R - 1)

    def send(src, dst, send_sem, recv_sem, device):
        pltpu.make_async_remote_copy(src, dst, send_sem, recv_sem, device_id=device, device_id_type=MESH).start()

    def each(count, fn):
        def body(i, carry):
            fn(i)
            return carry
        lax.fori_loop(1, count, body, 0)

    for b, (rs, zs) in enumerate(PIVOTS):
        @pl.when((r == rs) & (z == zs))
        def _():
            each(R, lambda i: send(x.at[0, 0, eight(lax.rem(rs + i, R))], piv.at[b, eight(lax.rem(rs + i, R))],
                                   s_a.at[b], r_a.at[b], at_row(i)))
            piv[b, 8 * rs : 8 * rs + 8, :] = x[0, 0, 8 * rs : 8 * rs + 8, :]

    for b in range(2):
        @pl.when(r == b)
        def _():
            each(R, lambda i: send(x.at[0, :, eight(lax.rem(b + i, R))], rb.at[b, :, eight(lax.rem(b + i, R))],
                                   s_1.at[b], r_1.at[b], at_row(i)))
            rb[b, :, 8 * b : 8 * b + 8, :] = x[0, :, 8 * b : 8 * b + 8, :]

    for b, (rs, zs) in enumerate(PIVOTS):
        mine = piv.at[b, eight(r)]

        @pl.when((z == zs) & (r != rs))
        def _():
            wait_for(mine, r_a.at[b])

        @pl.when(z == zs)
        def _():
            each(Z, lambda i: send(mine, mine, s_b.at[b], r_b.at[b], at_col(i)))

        @pl.when(z != zs)
        def _():
            wait_for(mine, r_b.at[b])

        each(R, lambda i: send(mine, mine, s_c.at[b], r_c.at[b], at_row(i)))

    for p in range(2):
        @pl.when(z == p)
        def _():
            cb[p, 0:NB, :] = x[0, 0]
            cb[p, NB : 2 * NB, :] = x[1, 0]

    def pump(chunk, p):
        zp = lax.rem(z + Z - p, Z)
        piece = cb.at[p, pl.ds(pl.multiple_of(chunk * ROWS, ROWS), ROWS)]

        @pl.when(zp != 0)
        def _():
            wait_for(piece, r_z.at[p, chunk])

        @pl.when(lax.rem(zp, 2) == 0)
        def _():
            forward = jnp.where(zp < 8, 2, jnp.where(zp == 10, -1, -2))
            back = jnp.where(zp == 0, -2, jnp.where(zp <= 8, -1, 1))

            @pl.when(zp != 8)
            def _():
                send(piece, piece, s_z.at[p], r_z.at[p, chunk], at_col(forward))

            send(piece, piece, s_z.at[p], r_z.at[p, chunk], at_col(back))

    for b in range(2):
        mine = rb.at[b, :, eight(r)]

        @pl.when(r != b)
        def _():
            wait_for(mine, r_1.at[b])

        each(R, lambda i: send(mine, mine, s_2.at[b], r_2.at[b], at_row(i)))

    all_but = pl.ds(0, 248)
    for b in range(3):
        wait_for(piv.at[b, all_but], r_c.at[b])

    w[...] = jnp.zeros_like(w)
    w[0:NB, 0:NB] = piv[0]
    w[0:NB, NB : 2 * NB] = piv[1]
    w[NB : 2 * NB, NB : 2 * NB] = piv[2]

    def step(k, carry):
        mine = pl.ds(pl.multiple_of(k * 128, 128), 128)
        window = pl.ds(pl.multiple_of(k * 128, 128), 640)
        factor128(w.at[mine, mine], ud.at[k], md, lambda i: pump(lax.rem(4 * k + i, 8), lax.div(k, 2)))
        w[mine, pl.ds(pl.multiple_of(512 + k * 128, 128), 128)] = jnp.where(
            lax.broadcasted_iota(jnp.int32, (128, 128), 0) == lax.broadcasted_iota(jnp.int32, (128, 128), 1), 1.0, 0.0)
        row = jnp.dot(md[...], w[mine, window], precision=HIGHEST)
        w[mine, window] = row

        def update(i, c):
            there = pl.ds(pl.multiple_of(i * 128, 128), 128)
            w[there, window] = w[there, window] - jnp.dot(w[mine, there].T, w[mine, window], precision=HIGHEST)
            return c

        lax.fori_loop(k + 1, 4, update, 0)
        return carry

    lax.fori_loop(0, 4, step, 0)

    for b in range(2):
        wait_for(rb.at[b, :, all_but], r_2.at[b])
    m0, m1 = w[0:NB, 512:768], w[NB : 2 * NB, 512:1024]
    nt = (((1,), (1,)), ((), ()))

    def solve_below(k, carry):
        here = pl.ds(pl.multiple_of(k * NB, NB), NB)
        c0, c1 = cb[0, here], cb[1, here]
        below[here, 0:NB] = lax.dot_general(c0, m0, nt, precision=HIGHEST)
        below[here, NB : 2 * NB] = (lax.dot_general(c0, m1[:, 0:NB], nt, precision=HIGHEST)
                                    + lax.dot_general(c1, m1[:, NB : 2 * NB], nt, precision=HIGHEST))
        return carry

    lax.fori_loop(0, 2, solve_below, 0)

    def solve_across(c, carry):
        r0, r1 = rb[0, c], rb[1, c]
        across[c, 0:NB] = jnp.dot(m0, r0, precision=HIGHEST)
        across[c, NB : 2 * NB] = (jnp.dot(m1[:, 0:NB], r0, precision=HIGHEST)
                                  + jnp.dot(m1[:, NB : 2 * NB], r1, precision=HIGHEST))
        return carry

    lax.fori_loop(0, 4, solve_across, 0)

    def product(i, carry):
        k, c = lax.div(i, 4), lax.rem(i, 4)
        here = pl.ds(pl.multiple_of(k * NB, NB), NB)
        bh, bl = split(below[here])
        ah, al = split(across[c])
        out[k, c] = x[k, c] - (dot(bh, ah) + dot(bh, al) + dot(bl, ah))
        return carry

    lax.fori_loop(0, 8, product, 0)

    for p in range(2):
        @pl.when(z == p)
        def _():
            for k in range(2):
                out[k, 0] = below[NB * k : NB * k + NB, NB * p : NB * p + NB]

    for p in range(2):
        @pl.when(r == p)
        def _():
            for c in range(1, 4):
                out[0, c] = jnp.zeros((NB, NB), jnp.float32)

            @pl.when(z > p)
            def _():
                out[0, 0] = jnp.zeros((NB, NB), jnp.float32)

            @pl.when(z == p)
            def _():
                out[0, 0, 0:128, 0:128] = ud[2 * p].T
                out[0, 0, 0:128, 128:256] = jnp.zeros((128, 128), jnp.float32)
                out[0, 0, 128:256, 0:128] = w[256 * p : 256 * p + 128, 256 * p + 128 : 256 * p + 256].T
                out[0, 0, 128:256, 128:256] = ud[2 * p + 1].T

    for b, (rs, zs) in enumerate(PIVOTS):
        @pl.when((r == rs) & (z == zs))
        def _():
            wait_for(piv.at[b, all_but], s_a.at[b])

        @pl.when(z == zs)
        def _():
            wait_for(piv.at[b, pl.ds(0, 120)], s_b.at[b])

        wait_for(piv.at[b, all_but], s_c.at[b])
    for b in range(2):
        @pl.when(r == b)
        def _():
            wait_for(rb.at[b, :, all_but], s_1.at[b])

        wait_for(rb.at[b, :, all_but], s_2.at[b])
    for p in range(2):
        zp = lax.rem(z + Z - p, Z)

        @pl.when(lax.rem(zp, 2) == 0)
        def _():
            wait_for(cb.at[p], s_z.at[p])

            @pl.when(zp != 8)
            def _():
                wait_for(cb.at[p], s_z.at[p])


def shards(hessian, masses, shift):
    row_index, col_index = lax.axis_index("row"), lax.axis_index("col")
    weight = 1.0 / jnp.sqrt(masses)
    row_weight = lax.dynamic_index_in_dim(weight.reshape(2, R, NB), row_index, 1, keepdims=False)
    col_weight = lax.dynamic_index_in_dim(weight.reshape(4, Z, NB), col_index, 1, keepdims=False)
    row_cells = (jnp.arange(2) * R + row_index)[:, None] * NB + jnp.arange(NB)[None, :]
    col_cells = (jnp.arange(4) * Z + col_index)[:, None] * NB + jnp.arange(NB)[None, :]
    on_diagonal = row_cells[:, None, :, None] == col_cells[None, :, None, :]
    matrix = hessian.transpose(0, 2, 1, 3) * row_weight[:, None, :, None] * col_weight[None, :, None, :]
    matrix = matrix + jnp.where(on_diagonal, shift[0], 0.0)
    dma = pltpu.SemaphoreType.DMA
    f32 = jnp.float32
    factored = pl.pallas_call(
        kernel,
        out_shape=jax.ShapeDtypeStruct((2, 4, NB, NB), f32),
        in_specs=[pl.BlockSpec(memory_space=pltpu.VMEM)],
        out_specs=pl.BlockSpec(memory_space=pltpu.VMEM),
        scratch_shapes=[
            pltpu.VMEM((3, NB, NB), f32),
            pltpu.VMEM((2, 4, NB, NB), f32),
            pltpu.VMEM((2, 512, NB), f32),
            pltpu.VMEM((512, 1024), f32),
            pltpu.VMEM((4, 128, 128), f32),
            pltpu.VMEM((128, 128), f32),
            pltpu.VMEM((512, 512), f32),
            pltpu.VMEM((4, 512, NB), f32),
            dma((3,)), dma((3,)), dma((3,)), dma((3,)), dma((3,)), dma((3,)),
            dma((2,)), dma((2,)), dma((2,)), dma((2,)),
            dma((2,)), dma((2, CHUNKS)),
        ],
        compiler_params=pltpu.CompilerParams(collective_id=0, has_side_effects=True, vmem_limit_bytes=48 * 2**20),
    )(matrix)
    return factored.transpose(0, 2, 1, 3)


def solution(mesh):
    placed = (P(None, "row", None, "col"), P(), P())
    return jax.shard_map(
        shards, mesh=mesh, in_specs=placed, out_specs=P(None, "row", None, "col"), check_vma=False
    )
```

time: 1530 us -> 115 us (0.08)
  the two profiles are of different devices: /device:TPU:1 before, /device:TPU:262 now
where the time goes in v1:
time: 115 us
  Pallas kernels  108 us (94%)
  local copies, waits for them, and re-layouts  3.6 us (3%)
  other arithmetic  2.33 us (2%)
    pallas_call x1, Pallas kernels, shards(): pl.pallas_call(kernel, out_shape=jax.ShapeDtypeStruct((2, 4, NB, NB), f32...  108 us
    transpose x1, local copies, waits for them, and re-layouts, shards(): return factored.transpose(0, 2, 1, 3)  2.67 us

profile of v1, /device:TPU:262, one launch (start us, length us, event | category | flops | bytes accessed | tf_op | source)
XLA Modules:
  0.0 114.8 jit_solution(9671920450518003920)
XLA Ops:
  0.7 0.1 iota_add_fusion.1
  0.7 0.1 iota_add_fusion
  0.8 0.9 sqrt.3
  1.8 2.2 %bitcast_add_fusion.x = f32[2,4,256,256]{3,2,1,0:T(8,128)S(1)} fusion(f32[2,256,4,256]{3,2,1,0:T(4,128)} %param.3, f32[]{:T(128)} %bitcast.10, s32[4,256]{1,0:T(4,128)S(1)} %iota_add_fusion, s32[2,256]{1,0:T(2,128)S(1)} %iota_add_fusion.1, f32[4,256]{1,0:T(4,128)S(1)} %bitcast.12, f32[2,256]{1,0:T(2,128)S(1)} %bitcast.13), kind=kLoop, calls=%fused_computation | loop fusion | flops 2621440 | bytes 4206596 | tf_op jit(solution)/shard_map/add | solution.py:328
  4.0 108.1 %shard_map.37 = f32[2,4,256,256]{3,2,1,0:T(8,128)S(1)} custom-call(f32[2,4,256,256]{3,2,1,0:T(8,128)S(1)} %bitcast_add_fusion.x), custom_call_target="tpu_custom_call" | custom-call | tf_op jit(solution)/shard_map/pallas_call | solution.py:331
  112.1 2.7 %copy.7 = f32[2,256,4,256]{3,2,1,0:T(4,128)} copy(f32[2,256,4,256]{3,1,2,0:T(8,128)S(1)} %bitcast.11) | data formatting | bytes 4194304 | tf_op jit(solution)/shard_map/transpose | solution.py:351
  (8 shorter events, 0.1 us)

commit v2 on v1

v2 whole, which is shorter than its diff:
```python
import functools

import jax
import jax.numpy as jnp
from jax import lax
from jax.experimental import pallas as pl
from jax.experimental.pallas import tpu as pltpu
from jax.sharding import PartitionSpec as P

MESH = pl.DeviceIdType.MESH
HIGHEST = lax.Precision.HIGHEST
Z, R = 16, 32
NB = 256
CHUNKS = 16
ROWS = 1024 // CHUNKS


def wait_for(ref, sem):
    pltpu.make_async_copy(ref, ref, sem).wait()


def lane(x, i):
    return jnp.broadcast_to(x[:, i : i + 1], (8, 128))


def sublane(x, i):
    return jnp.broadcast_to(x[i : i + 1, :], (8, x.shape[1]))


def tree_sum(terms):
    while len(terms) > 1:
        terms = [terms[i] + terms[i + 1] for i in range(0, len(terms), 2)]
    return terms[0]


def factor8(tile, off):
    s, low, inv = {}, {}, {}
    for k in range(8):
        column = lane(tile, off + k)
        for i in range(k, 8):
            s[i, k] = sublane(column, i)
    for j in range(8):
        root = lax.rsqrt(s[j, j])
        for i in range(j + 1, 8):
            low[i, j] = s[i, j] * root
        for k in range(j + 1, 8):
            for i in range(k, 8):
                s[i, k] = s[i, k] - low[i, j] * low[k, j]
        inv[j, j] = root
        for c in range(j):
            total = low[j, c] * inv[c, c]
            for k in range(c + 1, j):
                total = total + low[j, k] * inv[k, c]
            inv[j, c] = -(total * root)
    row = lax.broadcasted_iota(jnp.int32, (8, 128), 0)
    columns = []
    for c in range(8):
        x = jnp.zeros((8, 128), jnp.float32)
        for i in range(c, 8):
            x = jnp.where(row == i, inv[i, c], x)
        columns.append(x)
    return columns


def combine(columns, x):
    return tree_sum([columns[j] * sublane(x, j) for j in range(8)])


def factor128(block, inverse_ref, done):
    rows = lax.broadcasted_iota(jnp.int32, (8, 128), 0)
    lanes = lax.broadcasted_iota(jnp.int32, (8, 128), 1)
    d = [block[8 * t : 8 * t + 8, :] for t in range(16)]
    e = [jnp.where(lanes == rows + 8 * t, 1.0, 0.0) for t in range(16)]
    for t in range(16):
        columns = factor8(d[t], 8 * t)
        u = combine(columns, d[t])
        f = combine(columns, e[t])
        inverse_ref[8 * t : 8 * t + 8, :] = f
        done(t)
        if t == 15:
            break
        v = u.T
        ub = [sublane(u, j) for j in range(8)]
        fb = [sublane(f, j) for j in range(8)]
        for q in range(t + 1, 16):
            vq = v[8 * q : 8 * q + 8, :]
            g = [lane(vq, j) for j in range(8)]
            d[q] = d[q] - tree_sum([g[j] * ub[j] for j in range(8)])
            e[q] = e[q] - tree_sum([g[j] * fb[j] for j in range(8)])


def split(x):
    high = x.astype(jnp.bfloat16)
    return high, (x - high.astype(jnp.float32)).astype(jnp.bfloat16)


def dot(a, b):
    return jnp.dot(a, b, preferred_element_type=jnp.float32)


NAMES = {}
_TOTAL = 0
for _name, _count in (("x", 2), ("fc", 2), ("fb", 4), ("pc", 4), ("r1s", 2), ("r1r", 2), ("r2s", 2), ("r2r", 2), ("rfs", 2), ("rfr", 2),
                      ("as", 4), ("ar", 4), ("bs", 4), ("br", 4), ("cs", 4), ("cr", 4), ("ss", 4), ("sr", 4),
                      ("zs", 2), ("ps", 1), ("zr", 2 * CHUNKS)):
    NAMES[_name] = _TOTAL
    _TOTAL += _count
SEMAPHORES = _TOTAL


def rows16(i):
    return pl.ds(pl.multiple_of(16 * i, 16), 16)


def kernel(shift, h, masses, out, x, acc, rb, cb, fb, tb, w, g, wc, wr, bel, acr, mi, u, ut, sems, ready_z, ready_p, ready_b):
    r, z = lax.axis_index("row"), lax.axis_index("col")
    chip, core = lax.div(r, 2), lax.rem(r, 2)
    even = core == 0
    first = (r == 0) & (z == 0)
    second = (r == 1) & (z == 0)
    odd = core == 1
    sibling = (r + 1 - 2 * core, z)
    zp = [z, lax.rem(z + Z - 1, Z)]

    def sem(name, i=0):
        return sems.at[NAMES[name] + i]

    def col(offset, row=None):
        return (r if row is None else row, lax.rem(z + offset + Z, Z))

    def chip_at(i):
        return (2 * i + core, z)

    def send(src, dst, send_sem, recv_sem, device):
        pltpu.make_async_remote_copy(src, dst, send_sem, recv_sem, device_id=device, device_id_type=MESH).start()

    def signal(s, device):
        pl.semaphore_signal(s, inc=1, device_id=device, device_id_type=MESH)

    def each(low, high, fn):
        def body(i, carry):
            fn(i)
            return carry
        lax.fori_loop(low, high, body, 0)

    def pick(value, cases, default=0):
        result = default
        for key, v in cases.items():
            result = jnp.where(value == key, v, result)
        return result

    def children(p):
        v = zp[p]
        skip = {} if p == 1 else {15: -2}
        fwd = pick(v, {0: 1, 1: 2, 3: 2, 5: 2, 7: 1, 13: -2, 11: -2, 9: 1, **skip})
        back = pick(v, {0: -1, 3: -1, 5: -1, 7: -1, 13: 1, 11: 1})
        far = pick(v, {0: -3}) if p == 1 else None
        return fwd, back, far

    def parent(p):
        v = zp[p]
        offset = pick(v, {1: -1, 15: 1, 3: -2, 5: -2, 7: -2, 8: -1, 2: 1, 4: 1, 6: 1, 13: 2 if p == 0 else 3, 11: 2, 9: 2,
                          14: -1, 12: -1, 10: -1})
        slot = pick(v, {15: 1, 2: 1, 4: 1, 6: 1, 14: 1, 12: 1, 13: 0 if p == 0 else 2})
        return offset, slot

    kids = [children(0), children(1)]
    from_proxy = (r == 0) & ((z == 1) | (z == 15))

    barrier = pltpu.get_barrier_semaphore()
    signal(barrier, sibling)

    @pl.when(odd)
    def _():
        each(1, 16, lambda i: signal(barrier, chip_at(lax.rem(chip + i, 16))))

    @pl.when(odd & (chip != 0) & (z == 0))
    def _():
        signal(barrier, (0, 0))

    for p in range(2):
        own = even & jnp.logical_not(first) if p == 0 else even
        for offset in kids[p]:
            if offset is not None:
                @pl.when((offset != 0) & own)
                def _():
                    signal(barrier, col(offset))

    @pl.when(second)
    def _():
        signal(barrier, (0, 1))
        signal(barrier, (0, 15))

    @pl.when(odd & (z == 0))
    def _():
        each(1, Z, lambda i: signal(barrier, col(i)))

    one = jnp.int32(1)
    zero = jnp.int32(0)
    expected = (one + jnp.where(first, 15, 0) + jnp.where(odd, 15, 0)
                + jnp.where(even & (zp[0] != 0), one, zero) + jnp.where(even & (zp[1] != 0), one, zero) + jnp.where(odd & (z != 0), one, zero))

    def weights(block):
        return 1.0 / jnp.sqrt(masses[pl.ds(2 * block, 2), :])

    across_weights = [weights(z + Z * c) for c in range(4)]
    square = lax.broadcasted_iota(jnp.int32, (NB, NB), 0) == lax.broadcasted_iota(jnp.int32, (NB, NB), 1)
    for k in range(2):
        down = weights(r + R * k)
        for half in range(2):
            tall = jnp.broadcast_to(down[half : half + 1, :], (128, 128)).T
            rows = slice(128 * half, 128 * half + 128)
            for c in range(4):
                for side in range(2):
                    cols = slice(128 * side, 128 * side + 128)
                    x[k, c, rows, cols] = h[k, rows, c, cols] * tall * across_weights[c][side : side + 1, :]
        for c in range(4):
            @pl.when(r + R * k == z + Z * c)
            def _():
                x[k, c] = x[k, c] + jnp.where(square, shift[0], 0.0)

    pl.semaphore_wait(barrier, expected)

    for p in range(2):
        offset, slot = parent(p)
        for s in range(3 if p == 1 else 2):
            if p == 0:
                @pl.when(even & (zp[p] != 0) & (slot == s) & jnp.logical_not(from_proxy))
                def _():
                    signal(ready_z.at[p, s], col(offset))
            else:
                @pl.when(even & (zp[p] != 0) & (slot == s))
                def _():
                    signal(ready_z.at[p, s], col(offset))

    @pl.when((r == 0) & (z == 1))
    def _():
        signal(ready_p.at[0], (1, 0))

    @pl.when((r == 0) & (z == 15))
    def _():
        signal(ready_p.at[1], (1, 0))

    @pl.when(odd & (z != 0))
    def _():
        signal(ready_b, (r, 0))

    def chunk_of(i):
        return pl.ds(pl.multiple_of(i * ROWS, ROWS), ROWS)

    def chain_send(p, i, offset):
        piece = cb.at[p, chunk_of(i)]
        send(piece, piece, sem("zs", p), sem("zr", p * CHUNKS + i), col(offset))

    def all_chunks(p, slot, offset):
        pl.semaphore_wait(ready_z.at[p, slot], 1)
        each(0, CHUNKS, lambda i: chain_send(p, i, offset))

    def pumps(p, between=None):
        fwd, back, _ = kids[p]

        @pl.when(fwd != 0)
        def _():
            pl.semaphore_wait(ready_z.at[p, 0], 1)

        @pl.when(back != 0)
        def _():
            pl.semaphore_wait(ready_z.at[p, 1], 1)

        def pump(i):
            wait_for(cb.at[p, chunk_of(i)], sem("zr", p * CHUNKS + i))

            @pl.when(fwd != 0)
            def _():
                chain_send(p, i, fwd)

            @pl.when(back != 0)
            def _():
                chain_send(p, i, back)

        if between is None:
            each(0, CHUNKS, pump)
        else:
            each(0, CHUNKS // 2, pump)
            between()
            each(CHUNKS // 2, CHUNKS, pump)
        theirs = cb.at[p, pl.ds(512, 512)]
        send(theirs, cb.at[p, pl.ds(0, 512)], sem("pc", 2 * p), sem("pc", 2 * p + 1), sibling)

    def width(k):
        return pl.ds(0, 512 - 128 * k)

    def slab(k, i):
        return g.at[k, pl.ds(pl.multiple_of(8 * i, 8), 8), width(k)]

    def g_relay(k):
        piece = slab(k, chip)

        @pl.when(second)
        def _():
            wait_for(g.at[k, :, width(k)], sem("sr", k))

        @pl.when((z == 0) & (chip != 0))
        def _():
            wait_for(piece, sem("ar", k))

        @pl.when(z == 0)
        def _():
            if k == 0:
                pl.semaphore_wait(ready_b, Z - 1)
            each(1, Z, lambda i: send(piece, piece, sem("bs", k), sem("br", k), (r, 1 + lax.rem(i + 6, Z - 1))))

        @pl.when(z != 0)
        def _():
            wait_for(piece, sem("br", k))

        def spread(i):
            there = lax.rem(chip + i, 16)

            @pl.when((z != 0) | (there != 0))
            def _():
                send(piece, piece, sem("cs", k), sem("cr", k), chip_at(there))

        each(1, 16, spread)

    def g_arrive(k):
        whole = g.at[k, :, width(k)]

        @pl.when(jnp.logical_not(second))
        def _():
            wait_for(g.at[k, pl.ds(0, 120), width(k)], sem("cr", k))
            send(whole, whole, sem("ss", k), sem("sr", k), sibling)

    nt = (((1,), (1,)), ((), ()))

    def load_rows():
        for b in range(2):
            for c in range(4):
                wr[NB * b : NB * b + NB, NB * c : NB * c + NB] = rb[b, c]

    def invert(q):
        top, bottom = g[2 * q, :, 0:128], g[2 * q + 1, :, 0:128]
        mi[0:128, 0:128] = top
        mi[0:128, 128:256] = jnp.zeros((128, 128), jnp.float32)
        mi[128:256, 128:256] = bottom
        inner = jnp.dot(g[2 * q, :, 128:256].T, top, precision=HIGHEST)
        mi[128:256, 0:128] = -jnp.dot(bottom, inner, precision=HIGHEST)

    def solve_across(q):
        def body(c, carry):
            cols = pl.ds(pl.multiple_of(c * NB, NB), NB)
            acr[NB * q : NB * q + NB, cols] = jnp.dot(mi[...], wr[NB * q : NB * q + NB, cols], precision=HIGHEST)
            return carry
        lax.fori_loop(0, 4, body, 0)

    def solve_below(q):
        def body(k, carry):
            rows = pl.ds(pl.multiple_of(k * NB, NB), NB)
            here = slice(NB * q, NB * q + NB)
            bel[rows, here] = lax.dot_general(wc[rows, here], mi[...], nt, precision=HIGHEST)
            return carry
        lax.fori_loop(0, 2, body, 0)

    def update():
        u[0:128, :] = g[0, :, 256:512]
        u[128:256, :] = g[1, :, 128:384]
        ut[...] = u[...].T

        def below_part(k, carry):
            rows = pl.ds(pl.multiple_of(k * NB, NB), NB)
            wc[rows, NB : 2 * NB] = -jnp.dot(bel[rows, 0:NB], u[...], precision=HIGHEST)
            return carry
        lax.fori_loop(0, 2, below_part, 0)

        def across_part(c, carry):
            cols = pl.ds(pl.multiple_of(c * NB, NB), NB)
            wr[NB : 2 * NB, cols] = wr[NB : 2 * NB, cols] - jnp.dot(ut[...], acr[0:NB, cols], precision=HIGHEST)
            return carry
        lax.fori_loop(0, 4, across_part, 0)

    def product(q):
        def body(k, carry):
            rows = pl.ds(pl.multiple_of(k * NB, NB), NB)
            bh, bl = split(bel[rows, NB * q : NB * q + NB])
            for c in range(4):
                ah, al = split(acr[NB * q : NB * q + NB, NB * c : NB * c + NB])
                term = dot(bh, ah) + dot(bh, al) + dot(bl, ah)
                if q == 0:
                    acc[k, c] = x[k, c] - term
                else:
                    out[k, :, c, :] = acc[k, c] - term
            return carry
        lax.fori_loop(0, 2, body, 0)

    @pl.when(first)
    def _():
        send(x.at[0], rb.at[0], sem("x", 0), sem("x", 1), sibling)
        for k in range(2):
            send(x.at[k, 0], cb.at[0, pl.ds(NB * k, NB)], sem("fc", 0), sem("fc", 1), sibling)
        w[0:NB, 0:NB] = x[0, 0]

        def step(k, carry):
            mine = pl.ds(pl.multiple_of(k * 128, 128), 128)
            window = pl.ds(pl.multiple_of(k * 128 + 128, 128), 384)

            @pl.when(k == 2)
            def _():
                u[0:128, :] = g[0, :, 256:512]
                u[128:256, :] = g[1, :, 128:384]
                wait_for(fb.at[1], sem("fb", 3))
                w[NB : 2 * NB, NB : 2 * NB] = fb[1] - jnp.dot(u[...].T, u[...], precision=HIGHEST)

            def last(t):
                if t > 0:
                    @pl.when(k == 3)
                    def _():
                        send(slab(3, t), slab(3, t), sem("as", 3), sem("ar", 3), (2 * t + 1, z))

            factor128(w.at[mine, mine], g.at[k, :, pl.ds(0, 128)], last)

            @pl.when(k == 0)
            def _():
                wait_for(fb.at[0], sem("fb", 2))
                w[0:NB, NB : 2 * NB] = fb[0]

            @pl.when(k < 3)
            def _():
                g[k, :, 128:512] = jnp.dot(g[k, :, 0:128], w[mine, window], precision=HIGHEST)

            for n in range(4):
                @pl.when(k == n)
                def _():
                    if n < 3:
                        each(1, 16, lambda i: send(slab(n, i), slab(n, i), sem("as", n), sem("ar", n), (2 * i + 1, z)))
                    whole = g.at[n, :, width(n)]
                    send(whole, whole, sem("ss", n), sem("sr", n), sibling)

            @pl.when(lax.rem(k, 2) == 0)
            def _():
                there = pl.ds(pl.multiple_of(k * 128 + 128, 128), 128)
                w[there, window] = w[there, window] - jnp.dot(g[k, :, 128:256].T, g[k, :, 128:512], precision=HIGHEST)

            return carry

        lax.fori_loop(0, 4, step, 0)

    @pl.when((r == 0) & (z != 0))
    def _():
        send(x.at[0], rb.at[0], sem("x", 0), sem("x", 1), sibling)

    @pl.when(second)
    def _():
        tb[...] = x[0, 0].T
        send(tb, fb.at[0], sem("fb", 0), sem("fb", 2), sibling)

    for p in range(2):
        @pl.when((z == p) & (core == 1) & jnp.logical_not(second))
        def _():
            for k in range(2):
                send(x.at[k, 0], cb.at[p, pl.ds(512 + NB * k, NB)], sem("fc", 0), sem("fc", 1), sibling)

    @pl.when(r == 0)
    def _():
        rb[0] = x[0]

    @pl.when(r == 1)
    def _():
        rb[1] = x[0]

    def scatter(b):
        def body(i):
            piece = rb.at[b, :, rows16(i)]
            send(piece, piece, sem("r1s", b), sem("r1r", b), chip_at(i))
        each(1, 16, body)

    def gather(b):
        mine = rb.at[b, :, rows16(chip)]

        @pl.when(chip != 0)
        def _():
            wait_for(mine, sem("r1r", b))

        def spread(i):
            there = lax.rem(chip + i, 16)

            @pl.when(there != 0)
            def _():
                send(mine, mine, sem("r2s", b), sem("r2r", b), chip_at(there))

        each(1, 16, spread)

    @pl.when(r == 1)
    def _():
        scatter(1)
        wait_for(rb.at[0], sem("x", 1))
        scatter(0)

    def proxy(slot, device):
        pl.semaphore_wait(ready_p.at[slot], 1)

        def body(i):
            piece = cb.at[0, chunk_of(i)]
            send(piece, piece, sem("ps"), sem("zr", i), device)
        each(0, CHUNKS, body)

    @pl.when(second)
    def _():
        for k in range(2):
            cb[0, 512 + NB * k : 512 + NB * k + NB, :] = x[k, 0]
        wait_for(cb.at[0, pl.ds(0, 512)], sem("fc", 1))
        proxy(0, (0, 1))

    @pl.when(core == 1)
    def _():
        gather(1)
        gather(0)

    @pl.when(second)
    def _():
        proxy(1, (0, 15))

    for p in range(2):
        @pl.when((z == p) & even & jnp.logical_not(first))
        def _():
            for k in range(2):
                cb[p, NB * k : NB * k + NB, :] = x[k, 0]
            wait_for(cb.at[p, pl.ds(512, 512)], sem("fc", 1))

    @pl.when((z == 0) & even & jnp.logical_not(first))
    def _():
        all_chunks(0, 0, 1)
        all_chunks(0, 1, -1)

    @pl.when((z == 1) & even)
    def _():
        pl.semaphore_wait(ready_z.at[1, 1], 1)

        @pl.when(r == 0)
        def _():
            send(cb.at[1, pl.ds(512, NB)], fb.at[1], sem("fb", 1), sem("fb", 3), (0, 0))

        each(0, CHUNKS, lambda i: chain_send(1, i, -1))
        all_chunks(1, 0, 1)

    @pl.when((z == 1) & even)
    def _():
        pumps(0, lambda: all_chunks(1, 2, -3))

    @pl.when((z > 1) & even)
    def _():
        pumps(0)

    leaf = (kids[1][0] == 0) & (kids[1][1] == 0)

    @pl.when((z != 1) & even & jnp.logical_not(leaf))
    def _():
        pumps(1)

    def rows_arrive(b):
        @pl.when(core == 1)
        def _():
            @pl.when(chip != 0)
            def _():
                wait_for(rb.at[b, :, pl.ds(0, 240)], sem("r2r", b))

            if b == 0:
                @pl.when(chip != 0)
                def _():
                    send(rb.at[b], rb.at[b], sem("rfs", b), sem("rfr", b), sibling)
            else:
                send(rb.at[b], rb.at[b], sem("rfs", b), sem("rfr", b), sibling)

    late = z >= 3

    @pl.when(odd)
    def _():
        g_relay(0)
        g_relay(1)
        rows_arrive(1)
        rows_arrive(0)
        g_arrive(0)
        g_relay(2)
        g_arrive(1)

        @pl.when(late)
        def _():
            g_relay(3)
            g_arrive(2)
            g_arrive(3)

    @pl.when(even)
    def _():
        wait_for(rb.at[1], sem("rfr", 1))

        @pl.when(chip != 0)
        def _():
            wait_for(rb.at[0], sem("rfr", 0))

    load_rows()

    def load_column(p):
        @pl.when(odd & (z != p))
        def _():
            wait_for(cb.at[p, pl.ds(0, 512)], sem("pc", 2 * p + 1))

        here = slice(NB * p, NB * p + NB)
        for k in range(2):
            rows = slice(NB * k, NB * k + NB)
            old = wc[rows, here] if p else 0.0

            @pl.when(z == p)
            def _():
                wc[rows, here] = x[k, 0] + old

            @pl.when(z != p)
            def _():
                wc[rows, here] = cb[p, rows, :] + old

    load_column(0)

    def slabs_arrive(q):
        @pl.when(even & jnp.logical_not(first))
        def _():
            for k in (2 * q, 2 * q + 1):
                wait_for(g.at[k, :, width(k)], sem("sr", k))

    slabs_arrive(0)
    invert(0)
    solve_across(0)
    solve_below(0)
    update()
    product(0)

    @pl.when(odd & jnp.logical_not(late))
    def _():
        g_relay(3)
        g_arrive(2)
        g_arrive(3)

    @pl.when((z != 1) & even & leaf)
    def _():
        pumps(1)

    load_column(1)
    slabs_arrive(1)
    invert(1)
    solve_across(1)
    solve_below(1)
    product(1)

    tri = lax.broadcasted_iota(jnp.int32, (NB, NB), 0) >= lax.broadcasted_iota(jnp.int32, (NB, NB), 1)
    for p in range(2):
        @pl.when(z == p)
        def _():
            for k in range(2):
                out[k, :, 0, :] = bel[NB * k : NB * k + NB, NB * p : NB * p + NB]

    for p in range(2):
        @pl.when(r == p)
        def _():
            for c in range(1, 4):
                out[0, :, c, :] = jnp.zeros((NB, NB), jnp.float32)

            @pl.when(z > p)
            def _():
                out[0, :, 0, :] = jnp.zeros((NB, NB), jnp.float32)

            @pl.when(z == p)
            def _():
                out[0, :, 0, :] = jnp.where(tri, bel[0:NB, NB * p : NB * p + NB], 0.0)

    @pl.when(r == 0)
    def _():
        wait_for(x.at[0], sem("x", 0))

    @pl.when(first)
    def _():
        wait_for(cb.at[0, pl.ds(0, 512)], sem("fc", 0))
        for k in range(4):
            wait_for(g.at[k, pl.ds(0, 120), width(k)], sem("as", k))

    @pl.when(second)
    def _():
        wait_for(tb, sem("fb", 0))
        wait_for(rb, sem("ps"))

    for p in range(2):
        @pl.when((z == p) & (core == 1) & jnp.logical_not(second))
        def _():
            wait_for(cb.at[p, pl.ds(512, 512)], sem("fc", 0))

        @pl.when((z != p) & even)
        def _():
            wait_for(cb.at[p, pl.ds(0, 512)], sem("pc", 2 * p))

    @pl.when((r == 0) & (z == 1))
    def _():
        wait_for(fb.at[1], sem("fb", 1))

    for b in range(2):
        @pl.when(r == 1)
        def _():
            wait_for(rb.at[b, :, pl.ds(0, 240)], sem("r1s", b))
            wait_for(rb.at[b, :, pl.ds(0, 240)], sem("r2s", b))
            if b == 1:
                wait_for(rb.at[b], sem("rfs", b))

        @pl.when((core == 1) & (chip != 0))
        def _():
            wait_for(rb.at[b, :, pl.ds(0, 224)], sem("r2s", b))
            wait_for(rb.at[b], sem("rfs", b))

    for k in range(4):
        @pl.when(odd & (z == 0))
        def _():
            wait_for(g.at[k, pl.ds(0, 120), width(k)], sem("bs", k))

        @pl.when(odd & (z == 0) & (chip != 0))
        def _():
            wait_for(g.at[k, pl.ds(0, 112), width(k)], sem("cs", k))

        @pl.when(odd & ((z != 0) | (chip == 0)))
        def _():
            wait_for(g.at[k, pl.ds(0, 120), width(k)], sem("cs", k))

        @pl.when(first | (odd & jnp.logical_not(second)))
        def _():
            wait_for(g.at[k, :, width(k)], sem("ss", k))

    for p in range(2):
        own = even & jnp.logical_not(first) if p == 0 else even
        for offset in kids[p]:
            if offset is not None:
                @pl.when((offset != 0) & own)
                def _():
                    wait_for(cb.at[p], sem("zs", p))


def shards(hessian, masses, shift):
    f32 = jnp.float32
    vmem = pl.BlockSpec(memory_space=pltpu.VMEM)
    return pl.pallas_call(
        kernel,
        out_shape=jax.ShapeDtypeStruct(hessian.shape, f32),
        in_specs=[pl.BlockSpec(memory_space=pltpu.SMEM), vmem, vmem],
        out_specs=vmem,
        scratch_shapes=[
            pltpu.VMEM((2, 4, NB, NB), f32),
            pltpu.VMEM((2, 4, NB, NB), f32),
            pltpu.VMEM((2, 4, NB, NB), f32),
            pltpu.VMEM((2, 1024, NB), f32),
            pltpu.VMEM((2, NB, NB), f32),
            pltpu.VMEM((NB, NB), f32),
            pltpu.VMEM((512, 1024), f32),
            pltpu.VMEM((4, 128, 512), f32),
            pltpu.VMEM((512, 512), f32),
            pltpu.VMEM((512, 1024), f32),
            pltpu.VMEM((512, 512), f32),
            pltpu.VMEM((512, 1024), f32),
            pltpu.VMEM((NB, NB), f32),
            pltpu.VMEM((NB, NB), f32),
            pltpu.VMEM((NB, NB), f32),
            pltpu.SemaphoreType.DMA((SEMAPHORES,)),
            pltpu.SemaphoreType.REGULAR((2, 3)),
            pltpu.SemaphoreType.REGULAR((2,)),
            pltpu.SemaphoreType.REGULAR,
        ],
        compiler_params=pltpu.CompilerParams(collective_id=0, has_side_effects=True, vmem_limit_bytes=48 * 2**20),
    )(shift, hessian, masses.reshape(128, 128))


def solution(mesh):
    placed = (P(None, "row", None, "col"), P(), P())
    return jax.shard_map(
        shards, mesh=mesh, in_specs=placed, out_specs=P(None, "row", None, "col"), check_vma=False
    )
```

time: 115 us -> 77.1 us (0.67)
  the two profiles are of different devices: /device:TPU:262 before, /device:TPU:350 now
where the time goes in v2:
time: 77.1 us; the launch traced here: 76.9 us
  Pallas kernels  72.5 us (94%)
  local copies, waits for them, and re-layouts  3.74 us (5%)
    pallas_call x1, Pallas kernels, shards(): pl.pallas_call(kernel, out_shape=jax.ShapeDtypeStruct(hessian.shape, f32)...  72.5 us
    unnamed x5, local copies, waits for them, and re-layouts  3.74 us

profile of v2, /device:TPU:350, one launch (start us, length us, event | category | flops | bytes accessed | tf_op | source)
XLA Modules:
  0.0 76.9 jit_solution(2103168460072132100)
XLA Ops:
  0.7 0.0 copy-start
  0.7 1.6 %copy-done = f32[2,256,4,256]{3,2,1,0:T(4,128)S(1)} copy-done((f32[2,256,4,256]{3,2,1,0:T(4,128)S(1)}, f32[2,256,4,256]{3,2,1,0:T(4,128)}, u32[]{:S(2)}) %copy-start) | copy-done | bytes 2097176
  2.2 0.0 copy-start.1
  2.2 0.8 %copy-done.1 = f32[16384]{0:T(1024)S(1)} copy-done((f32[16384]{0:T(1024)S(1)}, f32[16384]{0:T(1024)}, u32[]{:S(2)}) %copy-start.1) | copy-done | bytes 65560
  3.1 72.5 %shard_map.37 = f32[2,256,4,256]{3,2,1,0:T(4,128)S(1)} custom-call(f32[1]{0:T(128)S(6)} %copy.5.shift, f32[2,256,4,256]{3,2,1,0:T(4,128)S(1)} %copy-done, f32[128,128]{1,0:T(8,128)S(1)} %bitcast.1), custom_call_target="tpu_custom_call" | custom-call | tf_op jit(solution)/shard_map/pallas_call | solution.py:742
  75.6 1.3 %copy.6 = f32[2,256,4,256]{3,2,1,0:T(4,128)} copy(f32[2,256,4,256]{3,2,1,0:T(4,128)S(1)} %shard_map.37) | data formatting | bytes 4194304
Async XLA Ops:
  0.7 1.6 %copy-start = (f32[2,256,4,256]{3,2,1,0:T(4,128)S(1)}, f32[2,256,4,256]{3,2,1,0:T(4,128)}, u32[]{:S(2)}) copy-start(f32[2,256,4,256]{3,2,1,0:T(4,128)} %h.1) | copy-start | bytes 6291460
  2.2 0.8 %copy-start.1 = (f32[16384]{0:T(1024)S(1)}, f32[16384]{0:T(1024)}, u32[]{:S(2)}) copy-start(f32[16384]{0:T(1024)} %param.4) | copy-start | bytes 196612

commit v3 on v2

--- a/solution.py
+++ b/solution.py
@@ -11,7 +11,7 @@
 HIGHEST = lax.Precision.HIGHEST
 Z, R = 16, 32
 NB = 256
-CHUNKS = 16
+CHUNKS = 32
 ROWS = 1024 // CHUNKS
 
 
@@ -66,7 +66,7 @@
     return tree_sum([columns[j] * sublane(x, j) for j in range(8)])
 
 
-def factor128(block, inverse_ref, done):
+def factor128(block, inverse_ref):
     rows = lax.broadcasted_iota(jnp.int32, (8, 128), 0)
     lanes = lax.broadcasted_iota(jnp.int32, (8, 128), 1)
     d = [block[8 * t : 8 * t + 8, :] for t in range(16)]
@@ -76,7 +76,6 @@
         u = combine(columns, d[t])
         f = combine(columns, e[t])
         inverse_ref[8 * t : 8 * t + 8, :] = f
-        done(t)
         if t == 15:
             break
         v = u.T
@@ -100,7 +99,7 @@
 
 NAMES = {}
 _TOTAL = 0
-for _name, _count in (("x", 2), ("fc", 2), ("fb", 4), ("pc", 4), ("r1s", 2), ("r1r", 2), ("r2s", 2), ("r2r", 2), ("rfs", 2), ("rfr", 2),
+for _name, _count in (("in", 2), ("x", 2), ("fc", 2), ("fb", 4), ("pc", 4), ("r1s", 2), ("r1r", 2), ("r2s", 2), ("r2r", 2), ("rfs", 2), ("rfr", 2),
                       ("as", 4), ("ar", 4), ("bs", 4), ("br", 4), ("cs", 4), ("cr", 4), ("ss", 4), ("sr", 4),
                       ("zs", 2), ("ps", 1), ("zr", 2 * CHUNKS)):
     NAMES[_name] = _TOTAL
@@ -112,7 +111,13 @@
     return pl.ds(pl.multiple_of(16 * i, 16), 16)
 
 
-def kernel(shift, h, masses, out, x, acc, rb, cb, fb, tb, w, g, wc, wr, bel, acr, mi, u, ut, sems, ready_z, ready_p, ready_b):
+def dot3(a, b):
+    ah, al = split(a)
+    bh, bl = split(b)
+    return dot(ah, bh) + dot(ah, bl) + dot(al, bh)
+
+
+def kernel(shift, h_in, masses_in, out, h, masses, x, acc, rb, cb, fb, tb, w, g, wc, wr, bel, acr, mi, u, ut, sems, ready_z, ready_p, ready_b):
     r, z = lax.axis_index("row"), lax.axis_index("col")
     chip, core = lax.div(r, 2), lax.rem(r, 2)
     even = core == 0
@@ -151,21 +156,26 @@
 
     def children(p):
         v = zp[p]
-        skip = {} if p == 1 else {15: -2}
-        fwd = pick(v, {0: 1, 1: 2, 3: 2, 5: 2, 7: 1, 13: -2, 11: -2, 9: 1, **skip})
+        near = {1: 2} if p == 1 else {15: -2}
+        fwd = pick(v, {0: 1, 3: 2, 5: 2, 7: 1, 13: -2, 11: -2, 9: 1, **near})
         back = pick(v, {0: -1, 3: -1, 5: -1, 7: -1, 13: 1, 11: 1})
-        far = pick(v, {0: -3}) if p == 1 else None
+        far = pick(v, {0: -3 if p == 1 else 3})
         return fwd, back, far
 
     def parent(p):
         v = zp[p]
-        offset = pick(v, {1: -1, 15: 1, 3: -2, 5: -2, 7: -2, 8: -1, 2: 1, 4: 1, 6: 1, 13: 2 if p == 0 else 3, 11: 2, 9: 2,
-                          14: -1, 12: -1, 10: -1})
-        slot = pick(v, {15: 1, 2: 1, 4: 1, 6: 1, 14: 1, 12: 1, 13: 0 if p == 0 else 2})
+        offset = pick(v, {1: -1, 15: 1, 3: -2 if p == 1 else -3, 5: -2, 7: -2, 8: -1, 2: 1, 4: 1, 6: 1,
+                          13: 3 if p == 1 else 2, 11: 2, 9: 2, 14: -1, 12: -1, 10: -1})
+        slot = pick(v, {15: 1, 2: 1, 4: 1, 6: 1, 14: 1, 12: 1, (13 if p == 1 else 3): 2})
         return offset, slot
 
     kids = [children(0), children(1)]
-    from_proxy = (r == 0) & ((z == 1) | (z == 15))
+    from_proxy = (r == 0) & ((z == 1) | (z == 3) | (z == 15))
+
+    load = pltpu.make_async_copy(h_in, h, sem("in", 0))
+    load.start()
+    load_masses = pltpu.make_async_copy(masses_in, masses, sem("in", 1))
+    load_masses.start()
 
     barrier = pltpu.get_barrier_semaphore()
     signal(barrier, sibling)
@@ -173,10 +183,6 @@
     @pl.when(odd)
     def _():
         each(1, 16, lambda i: signal(barrier, chip_at(lax.rem(chip + i, 16))))
-
-    @pl.when(odd & (chip != 0) & (z == 0))
-    def _():
-        signal(barrier, (0, 0))
 
     for p in range(2):
         own = even & jnp.logical_not(first) if p == 0 else even
@@ -190,6 +196,7 @@
     def _():
         signal(barrier, (0, 1))
         signal(barrier, (0, 15))
+        signal(barrier, (0, 3))
 
     @pl.when(odd & (z == 0))
     def _():
@@ -197,8 +204,41 @@
 
     one = jnp.int32(1)
     zero = jnp.int32(0)
-    expected = (one + jnp.where(first, 15, 0) + jnp.where(odd, 15, 0)
+    expected = (one + jnp.where(odd, 15, 0)
                 + jnp.where(even & (zp[0] != 0), one, zero) + jnp.where(even & (zp[1] != 0), one, zero) + jnp.where(odd & (z != 0), one, zero))
+
+    pl.semaphore_wait(barrier, expected)
+
+    for p in range(2):
+        offset, slot = parent(p)
+        for s in range(3):
+            if p == 0:
+                @pl.when(even & (zp[p] != 0) & (slot == s) & jnp.logical_not(from_proxy))
+                def _():
+                    signal(ready_z.at[p, s], col(offset))
+            else:
+                @pl.when(even & (zp[p] != 0) & (slot == s))
+                def _():
+                    signal(ready_z.at[p, s], col(offset))
+
+    @pl.when((r == 0) & (z == 1))
+    def _():
+        signal(ready_p.at[0], (1, 0))
+
+    @pl.when((r == 0) & (z == 15))
+    def _():
+        signal(ready_p.at[1], (1, 0))
+
+    @pl.when((r == 0) & (z == 3))
+    def _():
+        signal(ready_p.at[2], (1, 0))
+
+    @pl.when(odd & (z != 0))
+    def _():
+        signal(ready_b, (r, 0))
+
+    load_masses.wait()
+    load.wait()
 
     def weights(block):
         return 1.0 / jnp.sqrt(masses[pl.ds(2 * block, 2), :])
@@ -219,32 +259,6 @@
             def _():
                 x[k, c] = x[k, c] + jnp.where(square, shift[0], 0.0)
 
-    pl.semaphore_wait(barrier, expected)
-
-    for p in range(2):
-        offset, slot = parent(p)
-        for s in range(3 if p == 1 else 2):
-            if p == 0:
-                @pl.when(even & (zp[p] != 0) & (slot == s) & jnp.logical_not(from_proxy))
-                def _():
-                    signal(ready_z.at[p, s], col(offset))
-            else:
-                @pl.when(even & (zp[p] != 0) & (slot == s))
-                def _():
-                    signal(ready_z.at[p, s], col(offset))
-
-    @pl.when((r == 0) & (z == 1))
-    def _():
-        signal(ready_p.at[0], (1, 0))
-
-    @pl.when((r == 0) & (z == 15))
-    def _():
-        signal(ready_p.at[1], (1, 0))
-
-    @pl.when(odd & (z != 0))
-    def _():
-        signal(ready_b, (r, 0))
-
     def chunk_of(i):
         return pl.ds(pl.multiple_of(i * ROWS, ROWS), ROWS)
 
@@ -256,7 +270,7 @@
         pl.semaphore_wait(ready_z.at[p, slot], 1)
         each(0, CHUNKS, lambda i: chain_send(p, i, offset))
 
-    def pumps(p, between=None):
+    def pumps(p):
         fwd, back, _ = kids[p]
 
         @pl.when(fwd != 0)
@@ -278,12 +292,7 @@
             def _():
                 chain_send(p, i, back)
 
-        if between is None:
-            each(0, CHUNKS, pump)
-        else:
-            each(0, CHUNKS // 2, pump)
-            between()
-            each(CHUNKS // 2, CHUNKS, pump)
+        each(0, CHUNKS, pump)
         theirs = cb.at[p, pl.ds(512, 512)]
         send(theirs, cb.at[p, pl.ds(0, 512)], sem("pc", 2 * p), sem("pc", 2 * p + 1), sibling)
 
@@ -299,6 +308,7 @@
         @pl.when(second)
         def _():
             wait_for(g.at[k, :, width(k)], sem("sr", k))
+            each(1, 16, lambda i: send(slab(k, i), slab(k, i), sem("as", k), sem("ar", k), chip_at(i)))
 
         @pl.when((z == 0) & (chip != 0))
         def _():
@@ -333,10 +343,13 @@
 
     nt = (((1,), (1,)), ((), ()))
 
-    def load_rows():
-        for b in range(2):
-            for c in range(4):
-                wr[NB * b : NB * b + NB, NB * c : NB * c + NB] = rb[b, c]
+    def load_rows(b):
+        @pl.when(even & (chip != 0) if b == 0 else even)
+        def _():
+            wait_for(rb.at[b], sem("rfr", b))
+
+        for c in range(4):
+            wr[NB * b : NB * b + NB, NB * c : NB * c + NB] = rb[b, c]
 
     def invert(q):
         top, bottom = g[2 * q, :, 0:128], g[2 * q + 1, :, 0:128]
@@ -349,7 +362,7 @@
     def solve_across(q):
         def body(c, carry):
             cols = pl.ds(pl.multiple_of(c * NB, NB), NB)
-            acr[NB * q : NB * q + NB, cols] = jnp.dot(mi[...], wr[NB * q : NB * q + NB, cols], precision=HIGHEST)
+            acr[NB * q : NB * q + NB, cols] = dot3(mi[...], wr[NB * q : NB * q + NB, cols])
             return carry
         lax.fori_loop(0, 4, body, 0)
 
@@ -368,13 +381,13 @@
 
         def below_part(k, carry):
             rows = pl.ds(pl.multiple_of(k * NB, NB), NB)
-            wc[rows, NB : 2 * NB] = -jnp.dot(bel[rows, 0:NB], u[...], precision=HIGHEST)
+            wc[rows, NB : 2 * NB] = -dot3(bel[rows, 0:NB], u[...])
             return carry
         lax.fori_loop(0, 2, below_part, 0)
 
         def across_part(c, carry):
             cols = pl.ds(pl.multiple_of(c * NB, NB), NB)
-            wr[NB : 2 * NB, cols] = wr[NB : 2 * NB, cols] - jnp.dot(ut[...], acr[0:NB, cols], precision=HIGHEST)
+            wr[NB : 2 * NB, cols] = wr[NB : 2 * NB, cols] - dot3(ut[...], acr[0:NB, cols])
             return carry
         lax.fori_loop(0, 4, across_part, 0)
 
@@ -410,13 +423,7 @@
                 wait_for(fb.at[1], sem("fb", 3))
                 w[NB : 2 * NB, NB : 2 * NB] = fb[1] - jnp.dot(u[...].T, u[...], precision=HIGHEST)
 
-            def last(t):
-                if t > 0:
-                    @pl.when(k == 3)
-                    def _():
-                        send(slab(3, t), slab(3, t), sem("as", 3), sem("ar", 3), (2 * t + 1, z))
-
-            factor128(w.at[mine, mine], g.at[k, :, pl.ds(0, 128)], last)
+            factor128(w.at[mine, mine], g.at[k, :, pl.ds(0, 128)])
 
             @pl.when(k == 0)
             def _():
@@ -430,8 +437,6 @@
             for n in range(4):
                 @pl.when(k == n)
                 def _():
-                    if n < 3:
-                        each(1, 16, lambda i: send(slab(n, i), slab(n, i), sem("as", n), sem("ar", n), (2 * i + 1, z)))
                     whole = g.at[n, :, width(n)]
                     send(whole, whole, sem("ss", n), sem("sr", n), sibling)
 
@@ -491,9 +496,16 @@
 
     @pl.when(r == 1)
     def _():
-        scatter(1)
+        @pl.when(z == 0)
+        def _():
+            scatter(1)
+
         wait_for(rb.at[0], sem("x", 1))
         scatter(0)
+
+        @pl.when(z != 0)
+        def _():
+            scatter(1)
 
     def proxy(slot, device):
         pl.semaphore_wait(ready_p.at[slot], 1)
@@ -508,16 +520,17 @@
         for k in range(2):
             cb[0, 512 + NB * k : 512 + NB * k + NB, :] = x[k, 0]
         wait_for(cb.at[0, pl.ds(0, 512)], sem("fc", 1))
+        proxy(2, (0, 3))
+
+    @pl.when(odd)
+    def _():
+        gather(0)
+        gather(1)
+
+    @pl.when(second)
+    def _():
+        proxy(1, (0, 15))
         proxy(0, (0, 1))
-
-    @pl.when(core == 1)
-    def _():
-        gather(1)
-        gather(0)
-
-    @pl.when(second)
-    def _():
-        proxy(1, (0, 15))
 
     for p in range(2):
         @pl.when((z == p) & even & jnp.logical_not(first))
@@ -528,33 +541,31 @@
 
     @pl.when((z == 0) & even & jnp.logical_not(first))
     def _():
+        all_chunks(0, 2, 3)
+        all_chunks(0, 1, -1)
         all_chunks(0, 0, 1)
-        all_chunks(0, 1, -1)
 
     @pl.when((z == 1) & even)
     def _():
+        all_chunks(1, 0, 1)
         pl.semaphore_wait(ready_z.at[1, 1], 1)
 
         @pl.when(r == 0)
         def _():
             send(cb.at[1, pl.ds(512, NB)], fb.at[1], sem("fb", 1), sem("fb", 3), (0, 0))
 
+        all_chunks(1, 2, -3)
         each(0, CHUNKS, lambda i: chain_send(1, i, -1))
-        all_chunks(1, 0, 1)
-
-    @pl.when((z == 1) & even)
-    def _():
-        pumps(0, lambda: all_chunks(1, 2, -3))
-
-    @pl.when((z > 1) & even)
+
+    leaf = (kids[1][0] == 0) & (kids[1][1] == 0)
+
+    @pl.when((z != 1) & even & jnp.logical_not(leaf))
+    def _():
+        pumps(1)
+
+    @pl.when((z != 0) & even)
     def _():
         pumps(0)
-
-    leaf = (kids[1][0] == 0) & (kids[1][1] == 0)
-
-    @pl.when((z != 1) & even & jnp.logical_not(leaf))
-    def _():
-        pumps(1)
 
     def rows_arrive(b):
         @pl.when(core == 1)
@@ -570,33 +581,16 @@
             else:
                 send(rb.at[b], rb.at[b], sem("rfs", b), sem("rfr", b), sibling)
 
-    late = z >= 3
-
     @pl.when(odd)
     def _():
         g_relay(0)
         g_relay(1)
-        rows_arrive(1)
         rows_arrive(0)
         g_arrive(0)
         g_relay(2)
         g_arrive(1)
 
-        @pl.when(late)
-        def _():
-            g_relay(3)
-            g_arrive(2)
-            g_arrive(3)
-
-    @pl.when(even)
-    def _():
-        wait_for(rb.at[1], sem("rfr", 1))
-
-        @pl.when(chip != 0)
-        def _():
-            wait_for(rb.at[0], sem("rfr", 0))
-
-    load_rows()
+    load_rows(0)
 
     def load_column(p):
         @pl.when(odd & (z != p))
@@ -628,12 +622,25 @@
     invert(0)
     solve_across(0)
     solve_below(0)
+
+    @pl.when(odd)
+    def _():
+        rows_arrive(1)
+
+        @pl.when(z == 0)
+        def _():
+            g_relay(3)
+
+    load_rows(1)
     update()
     product(0)
 
-    @pl.when(odd & jnp.logical_not(late))
-    def _():
-        g_relay(3)
+    @pl.when(odd)
+    def _():
+        @pl.when(z != 0)
+        def _():
+            g_relay(3)
+
         g_arrive(2)
         g_arrive(3)
 
@@ -676,13 +683,14 @@
     @pl.when(first)
     def _():
         wait_for(cb.at[0, pl.ds(0, 512)], sem("fc", 0))
+
+    @pl.when(second)
+    def _():
         for k in range(4):
             wait_for(g.at[k, pl.ds(0, 120), width(k)], sem("as", k))
-
-    @pl.when(second)
-    def _():
         wait_for(tb, sem("fb", 0))
         wait_for(rb, sem("ps"))
+        wait_for(rb.at[0], sem("ps"))
 
     for p in range(2):
         @pl.when((z == p) & (core == 1) & jnp.logical_not(second))
@@ -739,12 +747,15 @@
 def shards(hessian, masses, shift):
     f32 = jnp.float32
     vmem = pl.BlockSpec(memory_space=pltpu.VMEM)
+    anywhere = pl.BlockSpec(memory_space=pltpu.HBM)
     return pl.pallas_call(
         kernel,
         out_shape=jax.ShapeDtypeStruct(hessian.shape, f32),
-        in_specs=[pl.BlockSpec(memory_space=pltpu.SMEM), vmem, vmem],
+        in_specs=[pl.BlockSpec(memory_space=pltpu.SMEM), anywhere, anywhere],
         out_specs=vmem,
         scratch_shapes=[
+            pltpu.VMEM(hessian.shape, f32),
+            pltpu.VMEM((128, 128), f32),
             pltpu.VMEM((2, 4, NB, NB), f32),
             pltpu.VMEM((2, 4, NB, NB), f32),
             pltpu.VMEM((2, 4, NB, NB), f32),
@@ -762,10 +773,10 @@
             pltpu.VMEM((NB, NB), f32),
             pltpu.SemaphoreType.DMA((SEMAPHORES,)),
             pltpu.SemaphoreType.REGULAR((2, 3)),
-            pltpu.SemaphoreType.REGULAR((2,)),
+            pltpu.SemaphoreType.REGULAR((3,)),
             pltpu.SemaphoreType.REGULAR,
         ],
-        compiler_params=pltpu.CompilerParams(collective_id=0, has_side_effects=True, vmem_limit_bytes=48 * 2**20),
+        compiler_params=pltpu.CompilerParams(collective_id=0, has_side_effects=True, vmem_limit_bytes=32 * 2**20),
     )(shift, hessian, masses.reshape(128, 128))
 
 

time: 77.1 us -> 71.6 us (0.929)
  the two profiles are of different devices: /device:TPU:350 before, /device:TPU:320 now
where the time goes in v3:
time: 71.6 us; the launch traced here: 71.4 us
  Pallas kernels  67 us (94%)
  local copies, waits for them, and re-layouts  3.74 us (5%)
    pallas_call x1, Pallas kernels, shards(): pl.pallas_call(kernel, out_shape=jax.ShapeDtypeStruct(hessian.shape, f32)...  67 us
    unnamed x5, local copies, waits for them, and re-layouts  3.74 us

profile of v3, /device:TPU:320, one launch (start us, length us, event | category | flops | bytes accessed | tf_op | source)
XLA Modules:
  0.0 71.4 jit_solution(7605467061218626805)
XLA Ops:
  0.7 0.0 copy-start
  0.7 1.6 %copy-done = f32[2,256,4,256]{3,2,1,0:T(4,128)S(1)} copy-done((f32[2,256,4,256]{3,2,1,0:T(4,128)S(1)}, f32[2,256,4,256]{3,2,1,0:T(4,128)}, u32[]{:S(2)}) %copy-start) | copy-done | bytes 2097176
  2.2 0.0 copy-start.1
  2.2 0.8 %copy-done.1 = f32[16384]{0:T(1024)S(1)} copy-done((f32[16384]{0:T(1024)S(1)}, f32[16384]{0:T(1024)}, u32[]{:S(2)}) %copy-start.1) | copy-done | bytes 65560
  3.1 67.0 %shard_map.37 = f32[2,256,4,256]{3,2,1,0:T(4,128)S(1)} custom-call(f32[1]{0:T(128)S(6)} %copy.5.shift, f32[2,256,4,256]{3,2,1,0:T(4,128)S(1)} %copy-done, f32[128,128]{1,0:T(8,128)S(1)} %bitcast.1), custom_call_target="tpu_custom_call" | custom-call | tf_op jit(solution)/shard_map/pallas_call | solution.py:751
  70.1 1.3 %copy.6 = f32[2,256,4,256]{3,2,1,0:T(4,128)} copy(f32[2,256,4,256]{3,2,1,0:T(4,128)S(1)} %shard_map.37) | data formatting | bytes 4194304
Async XLA Ops:
  0.7 1.6 %copy-start = (f32[2,256,4,256]{3,2,1,0:T(4,128)S(1)}, f32[2,256,4,256]{3,2,1,0:T(4,128)}, u32[]{:S(2)}) copy-start(f32[2,256,4,256]{3,2,1,0:T(4,128)} %h_in.1) | copy-start | bytes 6291460
  2.2 0.8 %copy-start.1 = (f32[16384]{0:T(1024)S(1)}, f32[16384]{0:T(1024)}, u32[]{:S(2)}) copy-start(f32[16384]{0:T(1024)} %param.4) | copy-start | bytes 196612
